TPU v7x, 32 devices: a whole 2x2x4 slice. The times are simulated.
32 devices in a mesh: groups: 2 (over y), dp: 4 (over z), tensor: 4 (over x, core).
Axes of the slice: x: 2, y: 2, z: 4, core: 2. Of those that a mesh axis runs over, the one named last changes fastest.
Arguments:
- remaining_members: int32 [32], P('groups'), parts along dimension 0, may hold values from 0 to 31, as said below
- allotment: int32 [64], P('groups'), parts along dimension 0, may hold values from 8 to 32
- sample_module_label: int32 [1024], P(('groups', 'dp')), parts along dimension 0, may hold values from 0 to 31, as said below
- block_source_vectors: bfloat16 [1024, 8192], P(('groups', 'dp'), 'tensor'), parts along dimension 0, may hold values from -6 to 6
- fixed_switch_projection: bfloat16 [1024, 28672], P(('groups', 'dp'), 'tensor'), parts along dimension 0, may hold values from -6 to 6
- fixed_expand_projection: bfloat16 [1024, 28672], P(('groups', 'dp'), 'tensor'), parts along dimension 0, may hold values from -6 to 6
- result_adjoint_vectors: bfloat16 [1024, 8192], P(('groups', 'dp'), 'tensor'), parts along dimension 0, may hold values from -6 to 6
- inner_activation_adjoint: bfloat16 [1024, 28672], P(('groups', 'dp'), 'tensor'), parts along dimension 0, may hold values from -6 to 6
- switch_left_matrices: bfloat16 [16384, 256], P(('groups', 'tensor'), 'dp'), parts along dimension 0, may hold values from -0.0625 to 0.0625
- switch_right_matrices: bfloat16 [512, 28672], P(('groups', 'dp'), 'tensor'), parts along dimension 0, may hold values from -0.29882812 to 0.29882812
- expand_left_matrices: bfloat16 [16384, 256], P(('groups', 'tensor'), 'dp'), parts along dimension 0, may hold values from -0.0625 to 0.0625
- expand_right_matrices: bfloat16 [512, 28672], P(('groups', 'dp'), 'tensor'), parts along dimension 0, may hold values from -0.29882812 to 0.29882812
- contract_left_matrices: bfloat16 [57344, 256], P(('groups', 'tensor'), 'dp'), parts along dimension 0, may hold values from -0.03125 to 0.03125
- contract_right_matrices: bfloat16 [512, 8192], P(('groups', 'dp'), 'tensor'), parts along dimension 0, may hold values from -0.29882812 to 0.29882812
Outputs:
- delta_out: bfloat16 [1024, 8192], P(('groups', 'dp'), 'tensor'), parts along dimension 0
- grad_x: bfloat16 [1024, 8192], P(('groups', 'dp'), 'tensor'), parts along dimension 0
- grad_a_gate: float32 [16384, 256], P(('groups', 'tensor'), 'dp'), parts along dimension 0
- gate_output_gradient: float32 [512, 28672], P(('groups', 'dp'), 'tensor'), parts along dimension 0
- grad_a_up: float32 [16384, 256], P(('groups', 'tensor'), 'dp'), parts along dimension 0
- up_output_gradient: float32 [512, 28672], P(('groups', 'dp'), 'tensor'), parts along dimension 0
- grad_a_down: float32 [57344, 256], P(('groups', 'tensor'), 'dp'), parts along dimension 0
- down_output_gradient: float32 [512, 8192], P(('groups', 'dp'), 'tensor'), parts along dimension 0
There are 2 independent parts, one for each index of `groups`. A program takes and returns all parts, laid end to end along the dimension named above; each array names one. Nothing has to cross between parts.
Inputs may be any that keep to these rules, and one draw needn't show every extreme that they name: `remaining_members`: distinct adapter ids. `sample_module_label`: every row names an adapter of the pruning list. Among the rows of one index of dp, the survivors at positions 4 * j to 4 * j + 3 of the list are named at most 32 times together, for every j, and exactly 32 times for some j.
All inputs are finite; a program needn't handle non-finite values.
Results may differ from a plain program's by a relative error of at most 0.0065.
Values may be sent and summed in bfloat16 or wider, within the bound.
A program may use at most 128 MiB of HBM per device.

v0:
```python
import jax
import jax.numpy as jnp
from jax import lax
from jax.sharding import PartitionSpec as P

RANK = 16


ADAPTER_SCALE = 2.0
WEIGHT_NUM = 16.0


def silu_slope(values):
    logistic = jax.nn.sigmoid(values)
    return logistic * (1.0 + values * (1.0 - logistic))


def select_rank(values, member):
    groups = member.shape[1]
    pieces = values.reshape(values.shape[0], groups, RANK)
    return jnp.sum(pieces * member[:, :, None], axis=1)


def spread_rank(values, member):
    groups = member.shape[1]
    widened = member[:, :, None] * values.astype(jnp.float32)[:, None, :]
    return widened.reshape(values.shape[0], groups * RANK).astype(jnp.bfloat16)


def leading_product(former, latter):
    return lax.dot_general(
        former, latter, (((0,), (0,)), ((), ())), preferred_element_type=jnp.float32
    )


def dot_last(former, latter):
    return lax.dot_general(
        former, latter, (((1,), (1,)), ((), ())), preferred_element_type=jnp.float32
    )


def on_device(
    remaining_members,
    allotment,
    sample_module_label,
    block_source_vectors,
    fixed_switch_projection,
    fixed_expand_projection,
    result_adjoint_vectors,
    inner_activation_adjoint,
    switch_left_matrices,
    switch_right_matrices,
    expand_left_matrices,
    expand_right_matrices,
    contract_left_matrices,
    contract_right_matrices,
):
    devices = lax.axis_size("dp")
    local_rows = sample_module_label.shape[0]
    capacity = max(local_rows // 8, local_rows // devices)
    device_row_count = switch_left_matrices.shape[1] // RANK
    entry_places = jnp.arange(remaining_members.shape[0], dtype=jnp.int32)
    retained_entry_place = jnp.sum(
        jnp.where(
            sample_module_label[:, None] == remaining_members[None, :], entry_places[None, :], 0
        ),
        axis=1,
    )
    adapter_ids = jnp.arange(allotment.shape[0], dtype=jnp.int32)
    row_quota = jnp.sum(
        jnp.where(sample_module_label[:, None] == adapter_ids[None, :], allotment[None, :], 0),
        axis=1,
    )
    token_row_weight = WEIGHT_NUM / row_quota.astype(jnp.float32)
    destination_device = retained_entry_place // device_row_count
    device_slot_index = retained_entry_place % device_row_count
    onehot_target = (
        destination_device[:, None] == jnp.arange(devices, dtype=jnp.int32)[None, :]
    ).astype(jnp.int32)
    earlier = jnp.cumsum(onehot_target, axis=0) - onehot_target
    rank_in = jnp.sum(earlier * onehot_target, axis=1)
    placing = destination_device * capacity + rank_in
    slot_total = devices * capacity

    def packed_rows(matrix):
        blank_buf = jnp.zeros((slot_total,) + matrix.shape[1:], matrix.dtype)
        return blank_buf.at[placing].set(matrix)

    cotangent_scaled_rows = (
        token_row_weight[:, None] * result_adjoint_vectors.astype(jnp.float32)
    ).astype(jnp.bfloat16)
    hid_scaled = (token_row_weight[:, None] * inner_activation_adjoint.astype(jnp.float32)).astype(
        jnp.bfloat16
    )
    slot_owner = jnp.full((slot_total,), -1, jnp.int32).at[placing].set(device_slot_index)
    outbound = (
        packed_rows(block_source_vectors),
        packed_rows(fixed_switch_projection),
        packed_rows(fixed_expand_projection),
        packed_rows(cotangent_scaled_rows),
        packed_rows(hid_scaled),
        slot_owner,
    )
    came_rows, arrived_gate, arrived_up_rows, arrived_cotangent, came_hid, came_owner = (
        lax.all_to_all(outbound[0], "dp", split_axis=0, concat_axis=0, tiled=True),
        lax.all_to_all(outbound[1], "dp", split_axis=0, concat_axis=0, tiled=True),
        lax.all_to_all(outbound[2], "dp", split_axis=0, concat_axis=0, tiled=True),
        lax.all_to_all(outbound[3], "dp", split_axis=0, concat_axis=0, tiled=True),
        lax.all_to_all(outbound[4], "dp", split_axis=0, concat_axis=0, tiled=True),
        lax.all_to_all(outbound[5], "dp", split_axis=0, concat_axis=0, tiled=True),
    )
    member = (came_owner[:, None] == jnp.arange(device_row_count, dtype=jnp.int32)[None, :]).astype(
        jnp.float32
    )
    part_gate = select_rank(
        jnp.dot(came_rows, switch_left_matrices, preferred_element_type=jnp.float32), member
    )
    part_up = select_rank(
        jnp.dot(came_rows, expand_left_matrices, preferred_element_type=jnp.float32), member
    )
    part_cot = select_rank(dot_last(arrived_cotangent, contract_right_matrices), member)
    low_gate, low_up = lax.psum((part_gate, part_up), "tensor")
    gate_rank_rows = low_gate.astype(jnp.bfloat16)
    up_rank_rows = low_up.astype(jnp.bfloat16)
    scattered_gate = spread_rank(gate_rank_rows, member)
    scattered_up_rows = spread_rank(up_rank_rows, member)
    gate_complete = arrived_gate.astype(jnp.float32) + ADAPTER_SCALE * jnp.dot(
        scattered_gate, switch_right_matrices, preferred_element_type=jnp.float32
    )
    up_complete = arrived_up_rows.astype(jnp.float32) + ADAPTER_SCALE * jnp.dot(
        scattered_up_rows, expand_right_matrices, preferred_element_type=jnp.float32
    )
    activated = gate_complete * jax.nn.sigmoid(gate_complete)
    hidden = (activated * up_complete).astype(jnp.bfloat16)
    low_hidden = lax.psum(
        select_rank(
            jnp.dot(hidden, contract_left_matrices, preferred_element_type=jnp.float32), member
        ),
        "tensor",
    )
    hidden_rank_rows = low_hidden.astype(jnp.bfloat16)
    scattered_hidden = spread_rank(hidden_rank_rows, member)
    delta_rows = (
        ADAPTER_SCALE
        * jnp.dot(scattered_hidden, contract_right_matrices, preferred_element_type=jnp.float32)
    ).astype(jnp.bfloat16)
    reduced_cotangent = lax.psum(part_cot, "tensor")
    cotangent_rank_rows = (ADAPTER_SCALE * reduced_cotangent).astype(jnp.bfloat16)
    down_output_gradient = ADAPTER_SCALE * leading_product(scattered_hidden, arrived_cotangent)
    spread_cot = spread_rank(cotangent_rank_rows, member)
    grad_a_down = leading_product(hidden, spread_cot)
    hidden_grad = came_hid.astype(jnp.float32) + dot_last(spread_cot, contract_left_matrices)
    gate_gradient_rows = (hidden_grad * up_complete * silu_slope(gate_complete)).astype(
        jnp.bfloat16
    )
    up_gradient_rows = (hidden_grad * activated).astype(jnp.bfloat16)
    gate_backward_pass, up_backward_pass = lax.psum(
        (
            select_rank(dot_last(gate_gradient_rows, switch_right_matrices), member),
            select_rank(dot_last(up_gradient_rows, expand_right_matrices), member),
        ),
        "tensor",
    )
    gate_backward_pass = (ADAPTER_SCALE * gate_backward_pass).astype(jnp.bfloat16)
    up_backward_pass = (ADAPTER_SCALE * up_backward_pass).astype(jnp.bfloat16)
    gate_output_gradient = ADAPTER_SCALE * leading_product(scattered_gate, gate_gradient_rows)
    up_output_gradient = ADAPTER_SCALE * leading_product(scattered_up_rows, up_gradient_rows)
    spread_back_gate = spread_rank(gate_backward_pass, member)
    spread_back_up = spread_rank(up_backward_pass, member)
    grad_a_gate = leading_product(came_rows, spread_back_gate)
    grad_a_up = leading_product(came_rows, spread_back_up)
    input_grad = (
        dot_last(spread_back_gate, switch_left_matrices)
        + dot_last(spread_back_up, expand_left_matrices)
    ).astype(jnp.bfloat16)
    delta_home, grad_home = (
        lax.all_to_all(delta_rows, "dp", split_axis=0, concat_axis=0, tiled=True),
        lax.all_to_all(input_grad, "dp", split_axis=0, concat_axis=0, tiled=True),
    )
    return (
        delta_home[placing],
        grad_home[placing],
        grad_a_gate,
        gate_output_gradient,
        grad_a_up,
        up_output_gradient,
        grad_a_down,
        down_output_gradient,
    )


def solution(mesh):
    in_specs = (
        P("groups"),
        P("groups"),
        P(("groups", "dp")),
        P(("groups", "dp"), "tensor"),
        P(("groups", "dp"), "tensor"),
        P(("groups", "dp"), "tensor"),
        P(("groups", "dp"), "tensor"),
        P(("groups", "dp"), "tensor"),
        P(("groups", "tensor"), "dp"),
        P(("groups", "dp"), "tensor"),
        P(("groups", "tensor"), "dp"),
        P(("groups", "dp"), "tensor"),
        P(("groups", "tensor"), "dp"),
        P(("groups", "dp"), "tensor"),
    )
    out_specs = (
        P(("groups", "dp"), "tensor"),
        P(("groups", "dp"), "tensor"),
        P(("groups", "tensor"), "dp"),
        P(("groups", "dp"), "tensor"),
        P(("groups", "tensor"), "dp"),
        P(("groups", "dp"), "tensor"),
        P(("groups", "tensor"), "dp"),
        P(("groups", "dp"), "tensor"),
    )
    return jax.shard_map(
        on_device, mesh=mesh, in_specs=in_specs, out_specs=out_specs, check_vma=False
    )
```

profile of v0, /device:TPU:24, one launch (start us, length us, event | category | flops | bytes accessed | tf_op | source)
XLA Modules:
  0.0 243.9 jit_solution(14563589224486482372)
XLA Ops:
  0.6 0.0 copy-start
  0.7 0.9 select_reduce_fusion.2
  1.6 0.1 fusion.20
  1.6 0.2 reduce_window_sum.11
  1.8 0.2 select_reduce_fusion
  2.0 1.0 scatter_custom_fusion
  3.0 0.7 all_to_all.56
  3.7 5.1 %all-to-all-start = ((s32[4,32,1]{1,2,0:T(1,128)}), s32[4,32,1]{1,2,0:T(1,128)S(1)}, u32[]{:S(2)}, u32[]{:S(2)}) async-start(s32[4,32,1]{1,2,0:T(1,128)} %bitcast.3), calls=%async_computation | async-start | bytes 4096 | tf_op jit(solution)/shard_map/all_to_all | solution.py:110
  8.8 2.7 %scatter_custom_fusion.2 = bf16[128,2048]{1,0:T(8,128)(2,1)} fusion(s32[128]{0:T(128)S(1)} %fusion.25, bf16[128,2048]{1,0:T(8,128)(2,1)} %param.17, bf16[]{:T(256)} %constant.49.clone.1), kind=kCustom, calls=%fused_computation.43 | custom fusion | bytes 524800 | tf_op jit(solution)/shard_map/scatter | solution.py:87
  11.4 6.3 %all-to-all-start.2 = ((bf16[4,32,2048]{2,1,0:T(8,128)(2,1)}), bf16[4,32,2048]{2,1,0:T(8,128)(2,1)S(1)}, u32[]{:S(2)}, u32[]{:S(2)}) async-start(bf16[4,32,2048]{2,1,0:T(8,128)(2,1)} %bitcast.6), calls=%async_computation.2 | async-start | bytes 1048576 | tf_op jit(solution)/shard_map/all_to_all | solution.py:105
  17.7 0.1 select_reduce_fusion.1
  17.8 2.2 scatter_custom_fusion.5
  20.0 8.7 %all-to-all-done.2 = bf16[4,32,2048]{2,1,0:T(8,128)(2,1)S(1)} async-done(((bf16[4,32,2048]{2,1,0:T(8,128)(2,1)}), bf16[4,32,2048]{2,1,0:T(8,128)(2,1)S(1)}, u32[]{:S(2)}, u32[]{:S(2)}) %all-to-all-start.2) | async-done | bytes 524320 | tf_op jit(solution)/shard_map/all_to_all | solution.py:105
  28.6 5.8 %all-to-all-start.6 = ((bf16[4,32,2048]{2,1,0:T(8,128)(2,1)}), bf16[4,32,2048]{2,1,0:T(8,128)(2,1)S(1)}, u32[]{:S(2)}, u32[]{:S(2)}) async-start(bf16[4,32,2048]{2,1,0:T(8,128)(2,1)} %bitcast.24), calls=%async_computation.6 | async-start | bytes 1048576 | tf_op jit(solution)/shard_map/all_to_all | solution.py:108
  34.5 5.3 %scatter_custom_fusion.3 = bf16[128,7168]{1,0:T(8,128)(2,1)} fusion(s32[128]{0:T(128)S(1)} %fusion.25, bf16[128,7168]{1,0:T(8,128)(2,1)} %param.19, bf16[]{:T(256)} %constant.49.clone.1), kind=kCustom, calls=%fused_computation.36 | custom fusion | bytes 1835520 | tf_op jit(solution)/shard_map/scatter | solution.py:87
  39.8 6.1 %all-to-all-done.6 = bf16[4,32,2048]{2,1,0:T(8,128)(2,1)S(1)} async-done(((bf16[4,32,2048]{2,1,0:T(8,128)(2,1)}), bf16[4,32,2048]{2,1,0:T(8,128)(2,1)S(1)}, u32[]{:S(2)}, u32[]{:S(2)}) %all-to-all-start.6) | async-done | bytes 524320 | tf_op jit(solution)/shard_map/all_to_all | solution.py:108
  45.9 0.8 copy-done.6
  46.7 5.9 %all-to-all-start.3 = ((bf16[4,32,7168]{2,1,0:T(8,128)(2,1)}), bf16[4,32,7168]{2,1,0:T(8,128)(2,1)S(1)}, u32[]{:S(2)}, u32[]{:S(2)}) async-start(bf16[4,32,7168]{2,1,0:T(8,128)(2,1)} %bitcast.100), calls=%async_computation.3 | async-start | bytes 3670016 | tf_op jit(solution)/shard_map/all_to_all | solution.py:107
  52.6 5.4 %scatter_custom_fusion.4 = bf16[128,7168]{1,0:T(8,128)(2,1)} fusion(s32[128]{0:T(128)S(1)} %fusion.25, bf16[128,7168]{1,0:T(8,128)(2,1)} %param.21, f32[128]{0:T(128)S(1)} %convert_divide_fusion, bf16[]{:T(256)} %constant.49.clone.1), kind=kCustom, calls=%fused_computation.26 | custom fusion | flops 2752512 | bytes 3670530 | tf_op jit(solution)/shard_map/scatter | solution.py:87
  58.0 34.3 %all-to-all-done.3 = bf16[4,32,7168]{2,1,0:T(8,128)(2,1)S(1)} async-done(((bf16[4,32,7168]{2,1,0:T(8,128)(2,1)}), bf16[4,32,7168]{2,1,0:T(8,128)(2,1)S(1)}, u32[]{:S(2)}, u32[]{:S(2)}) %all-to-all-start.3) | async-done | bytes 1835040 | tf_op jit(solution)/shard_map/all_to_all | solution.py:107
  92.3 6.8 %all-to-all-start.5 = ((bf16[4,32,7168]{2,1,0:T(8,128)(2,1)}), bf16[4,32,7168]{2,1,0:T(8,128)(2,1)}, u32[]{:S(2)}, u32[]{:S(2)}) async-start(bf16[4,32,7168]{2,1,0:T(8,128)(2,1)} %bitcast.99), calls=%async_computation.5 | async-start | bytes 3670016 | tf_op jit(solution)/shard_map/all_to_all | solution.py:109
  99.1 5.3 %scatter_custom_fusion.1 = bf16[128,7168]{1,0:T(8,128)(2,1)} fusion(s32[128]{0:T(128)S(1)} %fusion.25, bf16[128,7168]{1,0:T(8,128)(2,1)} %param.18, bf16[]{:T(256)} %constant.49.clone.1), kind=kCustom, calls=%fused_computation.38 | custom fusion | bytes 1835520 | tf_op jit(solution)/shard_map/scatter | solution.py:87
  104.4 34.5 %all-to-all-done.5 = bf16[4,32,7168]{2,1,0:T(8,128)(2,1)} async-done(((bf16[4,32,7168]{2,1,0:T(8,128)(2,1)}), bf16[4,32,7168]{2,1,0:T(8,128)(2,1)}, u32[]{:S(2)}, u32[]{:S(2)}) %all-to-all-start.5) | async-done | bytes 1835040 | tf_op jit(solution)/shard_map/all_to_all | solution.py:109
  138.9 6.8 %all-to-all-start.1 = ((bf16[4,32,7168]{2,1,0:T(8,128)(2,1)}), bf16[4,32,7168]{2,1,0:T(8,128)(2,1)}, u32[]{:S(2)}, u32[]{:S(2)}) async-start(bf16[4,32,7168]{2,1,0:T(8,128)(2,1)} %bitcast.98), calls=%async_computation.1 | async-start | bytes 3670016 | tf_op jit(solution)/shard_map/all_to_all | solution.py:106
  145.7 0.6 pad_clamp_fusion
  146.3 0.5 broadcast.234
  146.8 0.7 reduce.3
  147.5 0.1 eq.66
  147.6 1.3 fusion.7
  148.9 0.3 fusion.8
  149.2 2.0 fusion.9
  151.2 11.6 %all-reduce.1 = (f32[128,16]{0,1:T(8,128)}, bf16[128,16]{0,1:T(8,128)(2,1)}, bf16[128,16]{0,1:T(8,128)(2,1)}) all-reduce(f32[128,16]{0,1:T(8,128)} %fusion.9, f32[128,16]{0,1:T(8,128)S(1)} %fusion.7, f32[128,16]{0,1:T(8,128)S(1)} %fusion.8), channel_id=1, replica_groups=mesh['groups'=2,'dp'=4,'tensor'=4] {'tensor'}, use_global_device_ids=true, to_apply=%region_17.18 | all-reduce | flops 6144 | bytes 40960 | tf_op jit(solution)/shard_map/psum | solution.py:147
  162.8 0.7 convert_element_type.243
  163.5 0.7 convert_element_type.244
  164.2 0.7 fusion.21
  164.9 1.3 multiply_convert_fusion.11
  166.2 3.8 %fusion = f32[128,7168]{1,0:T(8,128)} fusion(bf16[128,64]{0,1:T(8,128)(2,1)S(1)} %bitcast.108, bf16[64,7168]{1,0:T(8,128)(2,1)} %param.25, bf16[128,7168]{1,0:T(8,128)(2,1)S(1)} %bitcast.97), kind=kOutput, calls=%fused_computation.10 | convolution fusion | flops 120193024 | bytes 6438912 | tf_op jit(solution)/shard_map/dot_general | solution.py:130
  170.0 4.0 %convolution_add_fusion = f32[128,7168]{1,0:T(8,128)} fusion(bf16[128,64]{0,1:T(8,128)(2,1)S(1)} %bitcast.106, bf16[7168,64]{0,1:T(8,128)(2,1)S(1)} %copy-done.8, bf16[128,7168]{1,0:T(8,128)(2,1)} %bitcast.39), kind=kOutput, calls=%fused_computation.8 | convolution fusion | flops 119275520 | bytes 6438912 | tf_op jit(solution)/shard_map/dot_general | solution.py:37
  174.0 11.6 %all-to-all-done.1 = bf16[4,32,7168]{2,1,0:T(8,128)(2,1)} async-done(((bf16[4,32,7168]{2,1,0:T(8,128)(2,1)}), bf16[4,32,7168]{2,1,0:T(8,128)(2,1)}, u32[]{:S(2)}, u32[]{:S(2)}) %all-to-all-start.1) | async-done | bytes 1835040 | tf_op jit(solution)/shard_map/all_to_all | solution.py:106
  185.6 5.0 %multiply_convert_fusion.1 = (bf16[128,7168]{1,0:T(8,128)(2,1)S(1)}, bf16[128,7168]{1,0:T(8,128)(2,1)S(1)}, bf16[128,7168]{1,0:T(8,128)(2,1)S(1)}) fusion(f32[128,7168]{1,0:T(8,128)} %convolution_add_fusion, f32[128,7168]{1,0:T(8,128)} %fusion, bf16[128,64]{0,1:T(8,128)(2,1)S(1)} %bitcast.119, bf16[64,7168]{1,0:T(8,128)(2,1)S(1)} %copy-done, ...), kind=kOutput, calls=%fused_computation.16 | convolution fusion | flops 133955584 | bytes 15613952 | tf_op jit(solution)/shard_map/dot_general | solution.py:127
  190.6 0.0 copy-start.3
  190.6 0.7 fusion.28
  191.4 0.0 copy-start.10
  191.4 0.8 fusion.29
  192.2 0.2 copy-done.3
  192.4 0.6 copy-done.4
  193.0 0.3 copy-done.10
  193.3 0.8 fusion.31
  194.1 10.3 %all-reduce = (bf16[128,16]{0,1:T(8,128)(2,1)S(1)}, f32[128,16]{0,1:T(8,128)S(1)}, f32[128,16]{0,1:T(8,128)S(1)}) all-reduce(f32[128,16]{0,1:T(8,128)S(1)} %get-tuple-element.9, f32[128,16]{0,1:T(8,128)S(1)} %get-tuple-element.10, f32[128,16]{0,1:T(8,128)S(1)} %get-tuple-element.8), channel_id=1, replica_groups=mesh['groups'=2,'dp'=4,'tensor'=4] {'tensor'}, use_global_device_ids=true, to_apply=%region_12.13 | all-reduce | flops 6144 | bytes 45056 | tf_op jit(solution)/shard_map/psum | solution.py:135
  204.4 0.3 fusion.30
  204.7 1.1 fusion.4
  205.8 5.9 %all-to-all-start.7 = ((bf16[4,32,2048]{2,1,0:T(8,128)(2,1)}), bf16[4,32,2048]{2,1,0:T(8,128)(2,1)S(1)}, u32[]{:S(2)}, u32[]{:S(2)}) async-start(bf16[4,32,2048]{2,1,0:T(8,128)(2,1)} %bitcast.33), calls=%async_computation.7 | async-start | bytes 1048576 | tf_op jit(solution)/shard_map/all_to_all | solution.py:178
  211.8 1.0 fusion.32
  212.8 1.1 fusion.3
  213.9 1.0 fusion.33
  214.9 1.6 convolution_multiply_fusion.2
  216.6 7.9 %all-to-all-done.7 = bf16[4,32,2048]{2,1,0:T(8,128)(2,1)S(1)} async-done(((bf16[4,32,2048]{2,1,0:T(8,128)(2,1)}), bf16[4,32,2048]{2,1,0:T(8,128)(2,1)S(1)}, u32[]{:S(2)}, u32[]{:S(2)}) %all-to-all-start.7) | async-done | bytes 524320 | tf_op jit(solution)/shard_map/all_to_all | solution.py:178
  224.4 5.8 %all-to-all-start.4 = ((bf16[4,32,2048]{2,1,0:T(8,128)(2,1)}), bf16[4,32,2048]{2,1,0:T(8,128)(2,1)S(1)}, u32[]{:S(2)}, u32[]{:S(2)}) async-start(bf16[4,32,2048]{2,1,0:T(8,128)(2,1)} %bitcast.20), calls=%async_computation.4 | async-start | bytes 1048576 | tf_op jit(solution)/shard_map/all_to_all | solution.py:177
  230.3 1.0 convolution_multiply_fusion.5
  231.3 3.3 %convolution_multiply_fusion.3 = f32[64,7168]{1,0:T(8,128)} fusion(bf16[128,64]{0,1:T(8,128)(2,1)S(1)} %bitcast.120, bf16[128,7168]{1,0:T(8,128)(2,1)} %copy-done.3), kind=kOutput, calls=%fused_computation.14 | convolution fusion | flops 117899264 | bytes 3686400 | tf_op jit(solution)/shard_map/dot_general | solution.py:31
  234.5 1.6 fusion.34
  236.2 1.8 gather_fusion.1
  238.0 4.1 %all-to-all-done.4 = bf16[4,32,2048]{2,1,0:T(8,128)(2,1)S(1)} async-done(((bf16[4,32,2048]{2,1,0:T(8,128)(2,1)}), bf16[4,32,2048]{2,1,0:T(8,128)(2,1)S(1)}, u32[]{:S(2)}, u32[]{:S(2)}) %all-to-all-start.4) | async-done | bytes 524320 | tf_op jit(solution)/shard_map/all_to_all | solution.py:177
  242.1 1.8 gather_fusion
  (46 shorter events, 0.2 us)
Async XLA Ops:
  0.6 184.9 %copy-start = (bf16[64,7168]{1,0:T(8,128)(2,1)S(1)}, bf16[64,7168]{1,0:T(8,128)(2,1)}, u32[]{:S(2)}) copy-start(bf16[64,7168]{1,0:T(8,128)(2,1)} %param.23) | copy-start | bytes 2752516
  0.6 17.0 %copy-start.20 = (s32[128]{0:T(128)S(1)}, s32[128]{0:T(128)}, u32[]{:S(2)}) copy-start(s32[128]{0:T(128)} %param.16) | copy-start | bytes 1540
  0.7 17.0 %copy-start.21 = (s32[32]{0:T(128)S(1)}, s32[32]{0:T(128)}, u32[]{:S(2)}) copy-start(s32[32]{0:T(128)} %param.15) | copy-start | bytes 388
  0.7 17.1 %copy-start.14 = (bf16[128,2048]{1,0:T(8,128)(2,1)S(1)}, bf16[128,2048]{1,0:T(8,128)(2,1)}, u32[]{:S(2)}) copy-start(bf16[128,2048]{1,0:T(8,128)(2,1)} %param.20) | copy-start | bytes 1572868
  3.7 7.7 %all-to-all-start = ((s32[4,32,1]{1,2,0:T(1,128)}), s32[4,32,1]{1,2,0:T(1,128)S(1)}, u32[]{:S(2)}, u32[]{:S(2)}) async-start(s32[4,32,1]{1,2,0:T(1,128)} %bitcast.3), calls=%async_computation | async-start | bytes 4096 | tf_op jit(solution)/shard_map/all_to_all | solution.py:110
  11.4 17.2 %all-to-all-start.2 = ((bf16[4,32,2048]{2,1,0:T(8,128)(2,1)}), bf16[4,32,2048]{2,1,0:T(8,128)(2,1)S(1)}, u32[]{:S(2)}, u32[]{:S(2)}) async-start(bf16[4,32,2048]{2,1,0:T(8,128)(2,1)} %bitcast.6), calls=%async_computation.2 | async-start | bytes 1048576 | tf_op jit(solution)/shard_map/all_to_all | solution.py:105
  28.6 17.3 %all-to-all-start.6 = ((bf16[4,32,2048]{2,1,0:T(8,128)(2,1)}), bf16[4,32,2048]{2,1,0:T(8,128)(2,1)S(1)}, u32[]{:S(2)}, u32[]{:S(2)}) async-start(bf16[4,32,2048]{2,1,0:T(8,128)(2,1)} %bitcast.24), calls=%async_computation.6 | async-start | bytes 1048576 | tf_op jit(solution)/shard_map/all_to_all | solution.py:108
  45.9 0.8 copy-start.6
  46.7 45.6 %all-to-all-start.3 = ((bf16[4,32,7168]{2,1,0:T(8,128)(2,1)}), bf16[4,32,7168]{2,1,0:T(8,128)(2,1)S(1)}, u32[]{:S(2)}, u32[]{:S(2)}) async-start(bf16[4,32,7168]{2,1,0:T(8,128)(2,1)} %bitcast.100), calls=%async_computation.3 | async-start | bytes 3670016 | tf_op jit(solution)/shard_map/all_to_all | solution.py:107
  92.3 46.6 %all-to-all-start.5 = ((bf16[4,32,7168]{2,1,0:T(8,128)(2,1)}), bf16[4,32,7168]{2,1,0:T(8,128)(2,1)}, u32[]{:S(2)}, u32[]{:S(2)}) async-start(bf16[4,32,7168]{2,1,0:T(8,128)(2,1)} %bitcast.99), calls=%async_computation.5 | async-start | bytes 3670016 | tf_op jit(solution)/shard_map/all_to_all | solution.py:109
  138.9 10.0 %copy-start.11 = (bf16[2048,64]{0,1:T(8,128)(2,1)S(1)}, bf16[2048,64]{0,1:T(8,128)(2,1)}, u32[]{:S(2)}) copy-start(bf16[2048,64]{0,1:T(8,128)(2,1)} %param.24) | copy-start | bytes 786436
  138.9 46.7 %all-to-all-start.1 = ((bf16[4,32,7168]{2,1,0:T(8,128)(2,1)}), bf16[4,32,7168]{2,1,0:T(8,128)(2,1)}, u32[]{:S(2)}, u32[]{:S(2)}) async-start(bf16[4,32,7168]{2,1,0:T(8,128)(2,1)} %bitcast.98), calls=%async_computation.1 | async-start | bytes 3670016 | tf_op jit(solution)/shard_map/all_to_all | solution.py:106
  147.6 1.6 copy-start.17
  166.2 3.8 %copy-start.15 = (bf16[128,4,16]{0,2,1:T(8,128)(2,1)}, bf16[128,4,16]{0,2,1:T(8,128)(2,1)S(1)}, u32[]{:S(2)}) copy-start(bf16[128,4,16]{0,2,1:T(8,128)(2,1)S(1)} %get-tuple-element.23) | copy-start | bytes 49156
  166.2 3.8 %copy-start.8 = (bf16[7168,64]{0,1:T(8,128)(2,1)S(1)}, bf16[7168,64]{0,1:T(8,128)(2,1)}, u32[]{:S(2)}) copy-start(bf16[7168,64]{0,1:T(8,128)(2,1)} %param.26) | copy-start | bytes 2752516
  170.0 15.6 %copy-start.19 = (bf16[128,4,16]{0,2,1:T(8,128)(2,1)S(1)}, bf16[128,4,16]{0,2,1:T(8,128)(2,1)}, u32[]{:S(2)}) copy-start(bf16[128,4,16]{0,2,1:T(8,128)(2,1)} %get-tuple-element.24) | copy-start | bytes 49156
  185.6 5.0 %copy-start.9 = (bf16[7168,64]{0,1:T(8,128)(2,1)S(1)}, bf16[7168,64]{0,1:T(8,128)(2,1)}, u32[]{:S(2)}) copy-start(bf16[7168,64]{0,1:T(8,128)(2,1)} %param.26) | copy-start | bytes 2752516
  190.6 1.6 copy-start.1
  190.6 1.8 copy-start.3
  190.6 2.4 copy-start.4
  191.4 1.9 copy-start.10
  192.4 1.6 copy-start.18
  192.4 12.0 %copy-start.13 = (bf16[2048,64]{0,1:T(8,128)(2,1)S(1)}, bf16[2048,64]{0,1:T(8,128)(2,1)}, u32[]{:S(2)}) copy-start(bf16[2048,64]{0,1:T(8,128)(2,1)} %param.22) | copy-start | bytes 786436
  204.7 8.1 %copy-start.12 = (bf16[64,2048]{1,0:T(8,128)(2,1)S(1)}, bf16[64,2048]{1,0:T(8,128)(2,1)}, u32[]{:S(2)}) copy-start(bf16[64,2048]{1,0:T(8,128)(2,1)} %param.27) | copy-start | bytes 786436
  205.8 9.1 %copy-start.16 = (bf16[128,4,16]{0,2,1:T(8,128)(2,1)S(1)}, bf16[128,4,16]{0,2,1:T(8,128)(2,1)}, u32[]{:S(2)}) copy-start(bf16[128,4,16]{0,2,1:T(8,128)(2,1)} %copy-done.15) | copy-start | bytes 49156
  205.8 18.6 %all-to-all-start.7 = ((bf16[4,32,2048]{2,1,0:T(8,128)(2,1)}), bf16[4,32,2048]{2,1,0:T(8,128)(2,1)S(1)}, u32[]{:S(2)}, u32[]{:S(2)}) async-start(bf16[4,32,2048]{2,1,0:T(8,128)(2,1)} %bitcast.33), calls=%async_computation.7 | async-start | bytes 1048576 | tf_op jit(solution)/shard_map/all_to_all | solution.py:178
  211.8 3.1 %copy-start.5 = (bf16[128,7168]{1,0:T(8,128)(2,1)S(1)}, bf16[128,7168]{1,0:T(8,128)(2,1)}, u32[]{:S(2)}) copy-start(bf16[128,7168]{1,0:T(8,128)(2,1)} %copy-done.4) | copy-start | bytes 5505028
  214.9 15.3 %copy-start.7 = (bf16[4,32,2048]{2,1,0:T(8,128)(2,1)S(1)}, bf16[4,32,2048]{2,1,0:T(8,128)(2,1)}, u32[]{:S(2)}) copy-start(bf16[4,32,2048]{2,1,0:T(8,128)(2,1)} %copy-done.6) | copy-start | bytes 1572868
  224.4 17.6 %all-to-all-start.4 = ((bf16[4,32,2048]{2,1,0:T(8,128)(2,1)}), bf16[4,32,2048]{2,1,0:T(8,128)(2,1)S(1)}, u32[]{:S(2)}, u32[]{:S(2)}) async-start(bf16[4,32,2048]{2,1,0:T(8,128)(2,1)} %bitcast.20), calls=%async_computation.4 | async-start | bytes 1048576 | tf_op jit(solution)/shard_map/all_to_all | solution.py:177
  231.3 3.3 %copy-start.2 = (bf16[128,7168]{1,0:T(8,128)(2,1)S(1)}, bf16[128,7168]{1,0:T(8,128)(2,1)}, u32[]{:S(2)}) copy-start(bf16[128,7168]{1,0:T(8,128)(2,1)} %copy-done.1) | copy-start | bytes 5505028
where the time goes:
time: 249 us; the launch traced here: 244 us
  waiting for transfers between devices  107 us (43%)
  starting transfers between devices  48.4 us (19%)
  matrix products  30.7 us (12%)
  blocking collectives  21.9 us (9%)
  local copies, waits for them, and re-layouts  21.2 us (9%)
  other arithmetic  13.7 us (6%)
    all_to_all x1, waiting for transfers between devices, on_device(): lax.all_to_all(outbound[4], 'dp', split_axis=0, concat_axis=0, tiled=True)  34.5 us
    all_to_all x1, waiting for transfers between devices, on_device(): lax.all_to_all(outbound[2], 'dp', split_axis=0, concat_axis=0, tiled=True)  34.3 us
    scatter x3, local copies, waits for them, and re-layouts, packed_rows(): return blank_buf.at[placing].set(matrix)  13.3 us
    psum x1, blocking collectives, on_device(): reduced_cotangent = lax.psum(part_cot, 'tensor')  11.6 us
    all_to_all x1, waiting for transfers between devices, on_device(): lax.all_to_all(outbound[1], 'dp', split_axis=0, concat_axis=0, tiled=True)  11.6 us
    psum x1, blocking collectives, on_device(): lax.psum(select_rank(jnp.dot(hidden, contract_left_matrices, preferred_el...  10.3 us
    dot_general x6, matrix products, leading_product(): lax.dot_general(former, latter, (((0,), (0,)), ((), ())), preferred_eleme...  9.56 us
    dot_general x6, matrix products, dot_last(): lax.dot_general(former, latter, (((1,), (1,)), ((), ())), preferred_eleme...  8.97 us
  transfers between devices with their start and end apart: 8, of which 7 were waited for; matrix products, arithmetic and copies ran while one was open for 21% of the time, Pallas kernels for 0%

commit v1 on v0

v1 whole, which is shorter than its diff:
```python
import functools

import jax
import jax.numpy as jnp
from jax import lax
from jax.experimental import pallas as pl
from jax.experimental.pallas import tpu as pltpu
from jax.sharding import PartitionSpec as P

RANK = 16
ADAPTER_SCALE = 2.0
WEIGHT_NUM = 16.0
PARTS = 7
AHEAD = 7
F32 = jnp.float32
BF16 = jnp.bfloat16
MESH = pl.DeviceIdType.MESH


def dot(a, b):
    return jnp.dot(a, b, preferred_element_type=F32)


def dot_nt(a, b):
    return lax.dot_general(a, b, (((1,), (1,)), ((), ())), preferred_element_type=F32)


def iota(shape, axis):
    return lax.broadcasted_iota(jnp.int32, shape, axis)


def one_hot(condition):
    return jnp.where(condition, 1.0, 0.0).astype(BF16)


def kernel(
    sizes,
    label_ref, member_ref, allot_ref,
    x_hbm, gate_hbm, up_hbm, cot_hbm, hid_hbm,
    ag_hbm, bg_hbm, au_hbm, bu_hbm, ad_hbm, bd_hbm,
    delta_hbm, gx_hbm, gag_hbm, gbg_hbm, gau_hbm, gbu_hbm, gad_hbm, gbd_hbm,
    x_in, cot_in, ff_in,
    ag, au, bd, bg, bu, ad,
    x_send, x_recv, cot_send, cot_recv, ff_send, ff_recv,
    low_recv, back_recv, home_send, home_recv,
    gag, gau, gbd, gbg, gbu, gad, delta, gx,
    place, place_t, sg, su, sc,
    in_sem, ffin_sem, out_sem, ffout_sem,
    xs_sem, xr_sem, fs_sem, fr_sem, ts_sem, tr_sem,
):
    dp, nt, cap = sizes
    slots = dp * cap
    rows, width = x_in.shape
    part = ff_in.shape[2] // 3
    ranks = ag.shape[0]
    kept = ranks // RANK
    sub = 256 if part % 256 == 0 else part
    me = lax.axis_index("dp")
    tme = lax.axis_index("tensor")
    barrier = pltpu.get_barrier_semaphore()
    for d in range(1, dp):
        pl.semaphore_signal(barrier, inc=1, device_id={"dp": lax.rem(me + d, dp)}, device_id_type=MESH)
    for d in range(1, nt):
        pl.semaphore_signal(barrier, inc=1, device_id={"tensor": lax.rem(tme + d, nt)}, device_id_type=MESH)

    first = [
        pltpu.make_async_copy(source, target, in_sem.at[n])
        for n, (source, target) in enumerate((
            (x_hbm, x_in), (cot_hbm, cot_in), (ag_hbm, ag), (au_hbm, au), (bd_hbm, bd),
            (bg_hbm, bg), (bu_hbm, bu), (ad_hbm, ad),
        ))
    ]

    def ff_load(k):
        at = pl.ds(pl.multiple_of(k * part, 128), part)
        return [
            pltpu.make_async_copy(
                source.at[:, at], ff_in.at[k, :, pl.ds(n * part, part)], ffin_sem.at[n, k]
            )
            for n, source in enumerate((gate_hbm, up_hbm, hid_hbm))
        ]

    first[0].start()
    first[1].start()

    @pl.loop(0, PARTS)
    def _(k):
        for copy in ff_load(k):
            copy.start()

    for copy in first[2:]:
        copy.start()

    label_col = jnp.transpose(jnp.broadcast_to(label_ref[...].astype(F32), (128, rows)))[:, :1]
    members = member_ref[...].astype(F32)
    n_surv = members.shape[1]
    pos_col = jnp.sum(
        jnp.where(label_col == members, iota((rows, n_surv), 1).astype(F32), 0.0), axis=1, keepdims=True
    )
    n_adapt = allot_ref.shape[1]
    quota = jnp.sum(
        jnp.where(label_col == iota((rows, n_adapt), 1).astype(F32), allot_ref[...].astype(F32), 0.0),
        axis=1, keepdims=True,
    )
    weight = WEIGHT_NUM / quota
    pos = jnp.transpose(jnp.broadcast_to(pos_col, (rows, 128)))[:8].astype(jnp.int32)[:1]
    wide = max(8, -(-dp // 8) * 8)
    dest_ids = iota((wide, rows), 0)
    chosen = (pos >= dest_ids * kept) & (pos < dest_ids * kept + kept)
    chosen_f = jnp.where(chosen, 1.0, 0.0)
    before = one_hot(iota((rows, rows), 0) < iota((rows, rows), 1))
    earlier = dot(chosen_f.astype(BF16), before)
    dest = jnp.sum(jnp.where(chosen, dest_ids.astype(F32), 0.0), axis=0, keepdims=True)
    rank = jnp.sum(chosen_f * earlier, axis=0, keepdims=True)
    placing = (dest * cap + rank).astype(jnp.int32)
    hot = jnp.where(iota((slots, rows), 0) == placing, 1.0, 0.0)
    place[...] = hot.astype(BF16)
    place_t[...] = jnp.transpose(hot).astype(BF16)
    own = pos - (dest * kept).astype(jnp.int32)
    lanes = iota((128, rows), 0)
    mask_home = one_hot((lanes >= own * RANK) & (lanes < own * RANK + RANK))

    def peer_copy(d, source, target, send_sem, recv_sem):
        peer = lax.rem(me + d, dp)
        return pltpu.make_async_remote_copy(
            src_ref=source(peer), dst_ref=target(me), send_sem=send_sem, recv_sem=recv_sem,
            device_id={"dp": peer}, device_id_type=MESH,
        )

    def x_copy(d):
        return peer_copy(d, lambda p: x_send.at[p], lambda p: x_recv.at[p], xs_sem.at[0, d], xr_sem.at[0, d])

    def cot_copy(d):
        return peer_copy(d, lambda p: cot_send.at[p], lambda p: cot_recv.at[p], xs_sem.at[1, d], xr_sem.at[1, d])

    def home_copy(d):
        return peer_copy(d, lambda p: home_send.at[p], lambda p: home_recv.at[p], xs_sem.at[2, d], xr_sem.at[2, d])

    def ff_copy(k, d):
        return peer_copy(
            d, lambda p: ff_send.at[k, p], lambda p: ff_recv.at[k, p], fs_sem.at[k, d], fr_sem.at[k, d]
        )

    def tensor_copy(which, buffer, d):
        peer = lax.rem(tme + d, nt)
        return pltpu.make_async_remote_copy(
            src_ref=buffer.at[tme], dst_ref=buffer.at[tme], send_sem=ts_sem.at[which, d],
            recv_sem=tr_sem.at[which, d], device_id={"tensor": peer}, device_id_type=MESH,
        )

    def by_device(values):
        return values.astype(BF16).reshape(dp, cap, values.shape[1])

    hot_rows = place[...]
    first[0].wait()
    x_send[:, :, 0:128] = by_device(dot_nt(hot_rows, mask_home))
    x_send[:, :, 128:] = by_device(dot(hot_rows, x_in[...]))
    pl.semaphore_wait(barrier, dp - 1 + nt - 1)
    for d in range(1, dp):
        x_copy(d).start()
    x_recv[me] = x_send[me]
    first[1].wait()
    cot_send[...] = by_device(dot(hot_rows, (weight * cot_in[...].astype(F32)).astype(BF16)))
    for d in range(1, dp):
        cot_copy(d).start()
    cot_recv[me] = cot_send[me]

    def send_part(k):
        for copy in ff_load(k):
            copy.wait()
        hot_now = place[...]
        for n in range(3):
            piece = ff_in[k, :, n * part:(n + 1) * part]
            if n == 2:
                piece = (weight * piece.astype(F32)).astype(BF16)
            ff_send[k, :, :, n * part:(n + 1) * part] = by_device(dot(hot_now, piece))
        for d in range(1, dp):
            ff_copy(k, d).start()
        ff_recv[k, me] = ff_send[k, me]

    @pl.loop(0, min(AHEAD, PARTS))
    def _(k):
        send_part(k)

    for copy in first[2:]:
        copy.wait()
    for d in range(1, dp):
        x_copy(d).wait_recv()
    mask = jnp.transpose(x_recv[:, :, 0:128].reshape(slots, 128).astype(F32))[:ranks]

    def select(values):
        masked = values * mask
        total = masked[0:RANK]
        for n in range(1, kept):
            total = total + masked[n * RANK:(n + 1) * RANK]
        return total

    def spread(values):
        return jnp.concatenate([values] * kept, axis=0) * mask

    x_rows = x_recv[:, :, 128:].reshape(slots, width)
    low_recv[tme, 0:RANK] = select(dot_nt(ag[...], x_rows))
    low_recv[tme, RANK:2 * RANK] = select(dot_nt(au[...], x_rows))
    for d in range(1, dp):
        cot_copy(d).wait_recv()
    low_recv[tme, 2 * RANK:] = select(dot_nt(bd[...], cot_recv[...].reshape(slots, width)))
    for d in range(1, nt):
        tensor_copy(0, low_recv, d).start()
    for d in range(1, nt):
        tensor_copy(0, low_recv, d).wait_recv()
    low = jnp.sum(low_recv[...], axis=0)
    sg_t = spread(low[0:RANK].astype(BF16).astype(F32))
    su_t = spread(low[RANK:2 * RANK].astype(BF16).astype(F32))
    sc_t = spread((ADAPTER_SCALE * low[2 * RANK:]).astype(BF16).astype(F32))
    sg[...] = jnp.transpose(sg_t).astype(BF16)
    su[...] = jnp.transpose(su_t).astype(BF16)
    sc[...] = jnp.transpose(sc_t).astype(BF16)
    sg_t, su_t, sc_t = sg_t.astype(BF16), su_t.astype(BF16), sc_t.astype(BF16)

    def ff_store(k):
        at = pl.ds(pl.multiple_of(k * part, 128), part)
        return [
            pltpu.make_async_copy(source.at[:, at], target.at[:, at], ffout_sem.at[n, k])
            for n, (source, target) in enumerate(((gbg, gbg_hbm), (gbu, gbu_hbm), (gad, gad_hbm)))
        ]

    def ff_part(k, totals):
        for d in range(1, dp):
            ff_copy(k, d).wait_recv()

        def ff_sub(j, totals):
            low_h, back_g, back_u = totals
            at = pl.ds(pl.multiple_of(k * part + j * sub, 128), sub)

            def piece(n):
                start = pl.multiple_of(n * part + j * sub, 128)
                return ff_recv[k, :, :, pl.ds(start, sub)].reshape(slots, sub).astype(F32)

            bg_now, bu_now, ad_now = bg[:, at], bu[:, at], ad[:, at]
            gate_full = piece(0) + ADAPTER_SCALE * dot(sg[...], bg_now)
            up_full = piece(1) + ADAPTER_SCALE * dot(su[...], bu_now)
            logistic = jax.nn.sigmoid(gate_full)
            activated = gate_full * logistic
            hidden = (activated * up_full).astype(BF16)
            hidden_grad = piece(2) + dot(sc[...], ad_now)
            slope = logistic * (1.0 + gate_full * (1.0 - logistic))
            gate_grad = (hidden_grad * up_full * slope).astype(BF16)
            up_grad = (hidden_grad * activated).astype(BF16)
            gbg[:, at] = ADAPTER_SCALE * dot(sg_t, gate_grad)
            gbu[:, at] = ADAPTER_SCALE * dot(su_t, up_grad)
            gad[:, at] = dot(sc_t, hidden)
            return (
                low_h + dot_nt(ad_now, hidden),
                back_g + dot_nt(bg_now, gate_grad),
                back_u + dot_nt(bu_now, up_grad),
            )

        totals = lax.fori_loop(0, part // sub, ff_sub, totals)
        for copy in ff_store(k):
            copy.start()
        if AHEAD < PARTS:
            @pl.when(k + AHEAD < PARTS)
            def _():
                send_part(k + AHEAD)
        return totals

    zero = jnp.zeros((ranks, slots), F32)
    low_h, back_g, back_u = lax.fori_loop(0, PARTS, ff_part, (zero, zero, zero))
    back_recv[tme, 0:RANK] = select(low_h)
    back_recv[tme, RANK:2 * RANK] = select(back_g)
    back_recv[tme, 2 * RANK:] = select(back_u)
    for d in range(1, nt):
        tensor_copy(1, back_recv, d).start()
    for d in range(1, nt):
        tensor_copy(1, back_recv, d).wait_recv()
    back = jnp.sum(back_recv[...], axis=0)
    sh_t = spread(back[0:RANK].astype(BF16).astype(F32))
    sbg_t = spread((ADAPTER_SCALE * back[RANK:2 * RANK]).astype(BF16).astype(F32))
    sbu_t = spread((ADAPTER_SCALE * back[2 * RANK:]).astype(BF16).astype(F32))
    sh = jnp.transpose(sh_t).astype(BF16)
    sbg = jnp.transpose(sbg_t).astype(BF16)
    sbu = jnp.transpose(sbu_t).astype(BF16)
    home_send[:, :, 0:width] = by_device(ADAPTER_SCALE * dot(sh, bd[...]))
    home_send[:, :, width:] = by_device(dot(sbg, ag[...]) + dot(sbu, au[...]))
    for d in range(1, dp):
        home_copy(d).start()
    home_recv[me] = home_send[me]
    gbd[...] = ADAPTER_SCALE * dot(sh_t.astype(BF16), cot_recv[...].reshape(slots, width))
    x_rows = x_recv[:, :, 128:].reshape(slots, width)
    gag[...] = dot(sbg_t.astype(BF16), x_rows)
    gau[...] = dot(sbu_t.astype(BF16), x_rows)
    last = [
        pltpu.make_async_copy(source, target, out_sem.at[n])
        for n, (source, target) in enumerate((
            (gbd, gbd_hbm), (gag, gag_hbm), (gau, gau_hbm), (delta, delta_hbm), (gx, gx_hbm)
        ))
    ]
    for copy in last[:3]:
        copy.start()
    for d in range(1, dp):
        home_copy(d).wait_recv()
    back_rows = place_t[...]
    delta[...] = dot(back_rows, home_recv[:, :, 0:width].reshape(slots, width)).astype(BF16)
    last[3].start()
    gx[...] = dot(back_rows, home_recv[:, :, width:].reshape(slots, width)).astype(BF16)
    last[4].start()

    for d in range(1, dp):
        x_copy(d).wait_send()
        cot_copy(d).wait_send()
        home_copy(d).wait_send()
    for d in range(1, nt):
        tensor_copy(0, low_recv, d).wait_send()
        tensor_copy(1, back_recv, d).wait_send()

    @pl.loop(0, PARTS)
    def _(k):
        for d in range(1, dp):
            ff_copy(k, d).wait_send()
        for copy in ff_store(k):
            copy.wait()

    for copy in last:
        copy.wait()


def on_device(
    remaining_members, allotment, sample_module_label, block_source_vectors,
    fixed_switch_projection, fixed_expand_projection, result_adjoint_vectors,
    inner_activation_adjoint, switch_left_matrices, switch_right_matrices,
    expand_left_matrices, expand_right_matrices, contract_left_matrices, contract_right_matrices,
):
    dp, nt = lax.axis_size("dp"), lax.axis_size("tensor")
    rows, width = block_source_vectors.shape
    hidden_units = fixed_switch_projection.shape[1]
    ranks = switch_right_matrices.shape[0]
    cap = max(rows // 8, rows // dp)
    slots = dp * cap
    part = hidden_units // PARTS

    def f32(*shape):
        return jax.ShapeDtypeStruct(shape, F32)

    anywhere = pl.BlockSpec(memory_space=pl.ANY)
    whole = pl.BlockSpec(memory_space=pltpu.VMEM)
    dma = pltpu.SemaphoreType.DMA
    outs = pl.pallas_call(
        functools.partial(kernel, (dp, nt, cap)),
        out_shape=(
            jax.ShapeDtypeStruct((rows, width), BF16),
            jax.ShapeDtypeStruct((rows, width), BF16),
            f32(ranks, width), f32(ranks, hidden_units),
            f32(ranks, width), f32(ranks, hidden_units),
            f32(ranks, hidden_units), f32(ranks, width),
        ),
        in_specs=[whole] * 3 + [anywhere] * 11,
        out_specs=[anywhere] * 8,
        scratch_shapes=[
            pltpu.VMEM((rows, width), BF16), pltpu.VMEM((rows, width), BF16),
            pltpu.VMEM((PARTS, rows, 3 * part), BF16),
            pltpu.VMEM((ranks, width), BF16), pltpu.VMEM((ranks, width), BF16),
            pltpu.VMEM((ranks, width), BF16),
            pltpu.VMEM((ranks, hidden_units), BF16), pltpu.VMEM((ranks, hidden_units), BF16),
            pltpu.VMEM((ranks, hidden_units), BF16),
            pltpu.VMEM((dp, cap, 128 + width), BF16), pltpu.VMEM((dp, cap, 128 + width), BF16),
            pltpu.VMEM((dp, cap, width), BF16), pltpu.VMEM((dp, cap, width), BF16),
            pltpu.VMEM((PARTS, dp, cap, 3 * part), BF16), pltpu.VMEM((PARTS, dp, cap, 3 * part), BF16),
            pltpu.VMEM((nt, 3 * RANK, slots), F32), pltpu.VMEM((nt, 3 * RANK, slots), F32),
            pltpu.VMEM((dp, cap, 2 * width), BF16), pltpu.VMEM((dp, cap, 2 * width), BF16),
            pltpu.VMEM((ranks, width), F32), pltpu.VMEM((ranks, width), F32),
            pltpu.VMEM((ranks, width), F32),
            pltpu.VMEM((ranks, hidden_units), F32), pltpu.VMEM((ranks, hidden_units), F32),
            pltpu.VMEM((ranks, hidden_units), F32),
            pltpu.VMEM((rows, width), BF16), pltpu.VMEM((rows, width), BF16),
            pltpu.VMEM((slots, rows), BF16), pltpu.VMEM((rows, slots), BF16),
            pltpu.VMEM((slots, ranks), BF16), pltpu.VMEM((slots, ranks), BF16),
            pltpu.VMEM((slots, ranks), BF16),
            dma((8,)), dma((3, PARTS)), dma((5,)), dma((3, PARTS)),
            dma((3, dp)), dma((3, dp)), dma((PARTS, dp)), dma((PARTS, dp)),
            dma((2, nt)), dma((2, nt)),
        ],
        compiler_params=pltpu.CompilerParams(
            collective_id=0, has_side_effects=True, vmem_limit_bytes=56 * 2**20
        ),
        cost_estimate=pl.CostEstimate(flops=3 * 10**9, bytes_accessed=20 * 2**20, transcendentals=10**6),
    )(
        sample_module_label.reshape(1, -1), remaining_members.reshape(1, -1), allotment.reshape(1, -1),
        block_source_vectors, fixed_switch_projection, fixed_expand_projection,
        result_adjoint_vectors, inner_activation_adjoint,
        switch_left_matrices.T, switch_right_matrices, expand_left_matrices.T,
        expand_right_matrices, contract_left_matrices.T, contract_right_matrices,
    )
    delta, gx, gag, gbg, gau, gbu, gad, gbd = outs
    return delta, gx, gag.T, gbg, gau.T, gbu, gad.T, gbd


def solution(mesh):
    rows = P(("groups", "dp"), "tensor")
    left = P(("groups", "tensor"), "dp")
    in_specs = (
        P("groups"), P("groups"), P(("groups", "dp")),
        rows, rows, rows, rows, rows,
        left, rows, left, rows, left, rows,
    )
    out_specs = (rows, rows, left, rows, left, rows, left, rows)
    return jax.shard_map(
        on_device, mesh=mesh, in_specs=in_specs, out_specs=out_specs, check_vma=False
    )
```

time: 249 us -> 191 us (0.77); the launches traced: 244 us -> 191 us
  Pallas kernels: 0 us -> 178 us
  waiting for transfers between devices: 107 us -> 0 us
  starting transfers between devices: 48.4 us -> 0 us
  matrix products: 30.7 us -> 0 us
  blocking collectives: 21.9 us -> 0 us
  other arithmetic: 13.7 us -> 0 us
  local copies, waits for them, and re-layouts: 21.2 us -> 12.5 us
    pallas_call x0 -> x1, Pallas kernels: none -> 178 us  [on_device(): pl.pallas_call(functools.partial(kernel, (dp, nt, cap)), out_shape=(jax.S...]
    all_to_all x8 -> x0, waiting for transfers between devices: 107 us -> none  [the longest x1 34.5 us: on_device(): lax.all_to_all(outbound[4], 'dp', split_axis=0, concat_axis=0, tiled=True)]
    all_to_all x8 -> x0, starting transfers between devices: 48.4 us -> none  [the longest x1 6.84 us: on_device(): lax.all_to_all(outbound[1], 'dp', split_axis=0, concat_axis=0, tiled=True)]
    dot_general x18 -> x0, matrix products: 30.7 us -> none  [the longest x6 9.56 us: leading_product(): lax.dot_general(former, latter, (((0,), (0,)), ((), ())), preferred_eleme...]
    psum x2 -> x0, blocking collectives: 21.9 us -> none  [the longest x1 11.6 us: on_device(): reduced_cotangent = lax.psum(part_cot, 'tensor')]
    scatter x4 -> x0, local copies, waits for them, and re-layouts: 14.3 us -> none  [the longest x3 13.3 us: packed_rows(): return blank_buf.at[placing].set(matrix)]
    unnamed x44 -> x18, local copies, waits for them, and re-layouts: 1.96 us -> 12.5 us
    scatter x2 -> x0, other arithmetic: 7.63 us -> none  [packed_rows(): return blank_buf.at[placing].set(matrix)]
  transfers between devices with their start and end apart: 8 -> 0, of which waited for: 7 -> 0; matrix products, arithmetic and copies ran while one was open for 21% -> 0% of each run, Pallas kernels for 0% -> 0%
where the time goes in v1:
time: 191 us
  Pallas kernels  178 us (93%)
  local copies, waits for them, and re-layouts  12.5 us (7%)
    pallas_call x1, Pallas kernels, on_device(): pl.pallas_call(functools.partial(kernel, (dp, nt, cap)), out_shape=(jax.S...  178 us
    unnamed x18, local copies, waits for them, and re-layouts  12.5 us

profile of v1, /device:TPU:24, one launch (start us, length us, event | category | flops | bytes accessed | tf_op | source)
XLA Modules:
  0.0 190.9 jit_solution(11833073081847020262)
XLA Ops:
  0.6 177.8 %shard_map.197 = (bf16[128,2048]{1,0:T(8,128)(2,1)}, bf16[128,2048]{1,0:T(8,128)(2,1)}, f32[64,2048]{1,0:T(8,128)}, f32[64,7168]{1,0:T(8,128)}, f32[64,2048]{1,0...) custom-call(s32[1,128]{1,0:T(1,128)} %bitcast.15, s32[1,16]{1,0:T(1,128)} %bitcast.16, ...), custom_call_target="tpu_custom_call" | custom-call | flops 3000000000 | bytes 20971520 | tf_op jit(solution)/shard_map/pallas_call | solution.py:347
  178.4 0.0 copy-start.2
  178.4 2.0 %copy.30 = bf16[128,2048]{1,0:T(8,128)(2,1)} copy(bf16[128,2048]{1,0:T(8,128)(2,1)} %get-tuple-element.32) | data formatting | bytes 1048576
  180.4 1.9 copy.31
  182.3 1.9 copy.32
  184.2 0.0 copy-done.2
  184.2 0.0 copy-start.4
  184.2 0.0 copy-start.1
  184.2 1.2 copy.33
  185.4 0.1 copy-done.4
  185.6 0.8 copy.34
  186.4 0.2 copy-done.1
  186.5 0.0 copy-start
  186.5 1.2 copy.35
  187.8 0.9 copy-done
  188.7 0.0 copy-start.3
  188.7 1.2 copy.36
  189.9 0.2 copy-done.3
  190.1 0.8 copy.37
Async XLA Ops:
  178.4 5.8 %copy-start.2 = (f32[64,7168]{1,0:T(8,128)S(1)}, f32[64,7168]{1,0:T(8,128)}, u32[]{:S(2)}) copy-start(f32[64,7168]{1,0:T(8,128)} %get-tuple-element.35) | copy-start | bytes 5505028
  184.2 1.4 copy-start.4
  184.2 2.3 %copy-start.1 = (f32[64,7168]{1,0:T(8,128)S(1)}, f32[64,7168]{1,0:T(8,128)}, u32[]{:S(2)}) copy-start(f32[64,7168]{1,0:T(8,128)} %get-tuple-element.37) | copy-start | bytes 5505028
  186.5 2.2 %copy-start = (f32[64,7168]{1,0:T(8,128)S(1)}, f32[64,7168]{1,0:T(8,128)}, u32[]{:S(2)}) copy-start(f32[64,7168]{1,0:T(8,128)} %get-tuple-element.22) | copy-start | bytes 5505028
  188.7 1.4 copy-start.3

commit v2 on v1

v2 whole, which is shorter than its diff:
```python
import functools

import jax
import jax.numpy as jnp
from jax import lax
from jax.experimental import pallas as pl
from jax.experimental.pallas import tpu as pltpu
from jax.sharding import PartitionSpec as P

RANK = 16
ADAPTER_SCALE = 2.0
WEIGHT_NUM = 16.0
PARTS = 7
F32 = jnp.float32
BF16 = jnp.bfloat16
MESH = pl.DeviceIdType.MESH


def dot(a, b):
    return jnp.dot(a, b, preferred_element_type=F32)


def dot_nt(a, b):
    return lax.dot_general(a, b, (((1,), (1,)), ((), ())), preferred_element_type=F32)


def iota(shape, axis):
    return lax.broadcasted_iota(jnp.int32, shape, axis)


def one_hot(condition):
    return jnp.where(condition, 1.0, 0.0).astype(BF16)


def kernel(
    sizes,
    label_hbm, member_hbm, allot_hbm,
    x_hbm, gate_hbm, up_hbm, cot_hbm, hid_hbm,
    ag_hbm, bg_hbm, au_hbm, bu_hbm, ad_hbm, bd_hbm,
    delta, gx, gag, gbg, gau, gbu, gad, gbd,
    label_ref, member_ref, allot_ref, x_in, cot_in, gu_in, hid_in,
    ag, au, bd, bg, bu, ad,
    x_send, x_recv, cot_send, cot_recv, gu_send, gu_recv, hid_send, hid_recv,
    low_recv, cot_sums, hidden_sums, back_recv,
    delta_send, delta_recv, gx_send, gx_recv, up_slope, acted,
    hiddens, place, place_t, sg, su, sc,
    in_sem, ffin_sem,
    xs_sem, xr_sem, fs_sem, fr_sem, ts_sem, tr_sem,
):
    dp, nt, cap = sizes
    slots = dp * cap
    rows, width = x_in.shape
    part = hid_in.shape[2]
    ranks = ag.shape[0]
    kept = ranks // RANK
    sub = 256 if part % 256 == 0 else part
    me = lax.axis_index("dp")
    tme = lax.axis_index("tensor")
    barrier = pltpu.get_barrier_semaphore()
    for d in range(1, dp):
        pl.semaphore_signal(barrier, inc=1, device_id={"dp": lax.rem(me + d, dp)}, device_id_type=MESH)
    for d in range(1, nt):
        pl.semaphore_signal(barrier, inc=1, device_id={"tensor": lax.rem(tme + d, nt)}, device_id_type=MESH)

    first = [
        pltpu.make_async_copy(source, target, in_sem.at[n])
        for n, (source, target) in enumerate((
            (x_hbm, x_in), (cot_hbm, cot_in), (ag_hbm, ag), (au_hbm, au), (bd_hbm, bd),
            (bg_hbm, bg), (bu_hbm, bu), (ad_hbm, ad),
        ))
    ]
    plan = [
        pltpu.make_async_copy(source, target, in_sem.at[8 + n])
        for n, (source, target) in enumerate((
            (label_hbm, label_ref), (member_hbm, member_ref), (allot_hbm, allot_ref),
        ))
    ]
    for copy in plan:
        copy.start()

    def gu_load(k):
        at = pl.ds(pl.multiple_of(k * part, 128), part)
        return [
            pltpu.make_async_copy(
                source.at[:, at], gu_in.at[k, :, pl.ds(n * part, part)], ffin_sem.at[n, k]
            )
            for n, source in enumerate((gate_hbm, up_hbm))
        ]

    def hid_load(k):
        at = pl.ds(pl.multiple_of(k * part, 128), part)
        return pltpu.make_async_copy(hid_hbm.at[:, at], hid_in.at[k], ffin_sem.at[2, k])

    first[0].start()

    @pl.loop(0, PARTS)
    def _(k):
        for copy in gu_load(k):
            copy.start()

    first[1].start()

    @pl.loop(0, PARTS)
    def _(k):
        hid_load(k).start()

    for copy in first[2:]:
        copy.start()

    for copy in plan:
        copy.wait()
    label_col = jnp.transpose(jnp.broadcast_to(label_ref[...].astype(F32), (128, rows)))[:, :1]
    members = member_ref[...].astype(F32)
    n_surv = members.shape[1]
    pos_col = jnp.sum(
        jnp.where(label_col == members, iota((rows, n_surv), 1).astype(F32), 0.0), axis=1, keepdims=True
    )
    n_adapt = allot_ref.shape[1]
    quota = jnp.sum(
        jnp.where(label_col == iota((rows, n_adapt), 1).astype(F32), allot_ref[...].astype(F32), 0.0),
        axis=1, keepdims=True,
    )
    weight = WEIGHT_NUM / quota
    pos = jnp.transpose(jnp.broadcast_to(pos_col, (rows, 128)))[:8].astype(jnp.int32)[:1]
    wide = max(8, -(-dp // 8) * 8)
    dest_ids = iota((wide, rows), 0)
    chosen = (pos >= dest_ids * kept) & (pos < dest_ids * kept + kept)
    chosen_f = jnp.where(chosen, 1.0, 0.0)
    before = one_hot(iota((rows, rows), 0) < iota((rows, rows), 1))
    earlier = dot(chosen_f.astype(BF16), before)
    dest = jnp.sum(jnp.where(chosen, dest_ids.astype(F32), 0.0), axis=0, keepdims=True)
    rank = jnp.sum(chosen_f * earlier, axis=0, keepdims=True)
    placing = (dest * cap + rank).astype(jnp.int32)
    hot = jnp.where(iota((slots, rows), 0) == placing, 1.0, 0.0)
    place[...] = hot.astype(BF16)
    place_t[...] = jnp.transpose(hot).astype(BF16)
    own = pos - (dest * kept).astype(jnp.int32)
    lanes = iota((128, rows), 0)
    mask_home = one_hot((lanes >= own * RANK) & (lanes < own * RANK + RANK))

    def peer_copy(d, source, target, send_sem, recv_sem):
        peer = lax.rem(me + d, dp)
        return pltpu.make_async_remote_copy(
            src_ref=source(peer), dst_ref=target(me), send_sem=send_sem, recv_sem=recv_sem,
            device_id={"dp": peer}, device_id_type=MESH,
        )

    def x_copy(d):
        return peer_copy(d, lambda p: x_send.at[p], lambda p: x_recv.at[p], xs_sem.at[0, d], xr_sem.at[0, d])

    def cot_copy(d):
        return peer_copy(d, lambda p: cot_send.at[p], lambda p: cot_recv.at[p], xs_sem.at[1, d], xr_sem.at[1, d])

    def delta_copy(d):
        return peer_copy(d, lambda p: delta_send.at[p], lambda p: delta_recv.at[p], xs_sem.at[2, d], xr_sem.at[2, d])

    def gx_copy(d):
        return peer_copy(d, lambda p: gx_send.at[p], lambda p: gx_recv.at[p], xs_sem.at[3, d], xr_sem.at[3, d])

    def gu_copy(k, d):
        return peer_copy(
            d, lambda p: gu_send.at[k, p], lambda p: gu_recv.at[k, p], fs_sem.at[0, k, d], fr_sem.at[0, k, d]
        )

    def hid_copy(k, d):
        return peer_copy(
            d, lambda p: hid_send.at[k, p], lambda p: hid_recv.at[k, p], fs_sem.at[1, k, d], fr_sem.at[1, k, d]
        )

    def tensor_copy(which, buffer, d):
        peer = lax.rem(tme + d, nt)
        return pltpu.make_async_remote_copy(
            src_ref=buffer.at[tme], dst_ref=buffer.at[tme], send_sem=ts_sem.at[which, d],
            recv_sem=tr_sem.at[which, d], device_id={"tensor": peer}, device_id_type=MESH,
        )

    def by_device(values):
        return values.astype(BF16).reshape(dp, cap, values.shape[1])

    hot_rows = place[...]
    first[0].wait()
    x_send[:, :, 0:128] = by_device(dot_nt(hot_rows, mask_home))
    x_send[:, :, 128:] = by_device(dot(hot_rows, x_in[...]))
    pl.semaphore_wait(barrier, dp - 1 + nt - 1)
    for d in range(1, dp):
        x_copy(d).start()
    x_recv[me] = x_send[me]

    @pl.loop(0, PARTS)
    def _(k):
        for copy in gu_load(k):
            copy.wait()
        gu_send[k] = by_device(dot(place[...], gu_in[k]))
        for d in range(1, dp):
            gu_copy(k, d).start()
        gu_recv[k, me] = gu_send[k, me]

    first[1].wait()
    cot_send[...] = by_device(dot(hot_rows, (weight * cot_in[...].astype(F32)).astype(BF16)))
    for d in range(1, dp):
        cot_copy(d).start()
    cot_recv[me] = cot_send[me]

    @pl.loop(0, PARTS)
    def _(k):
        hid_load(k).wait()
        hid_send[k] = by_device(dot(place[...], (weight * hid_in[k].astype(F32)).astype(BF16)))
        for d in range(1, dp):
            hid_copy(k, d).start()
        hid_recv[k, me] = hid_send[k, me]

    for copy in first[2:]:
        copy.wait()
    for d in range(1, dp):
        x_copy(d).wait_recv()
    mask = jnp.transpose(x_recv[:, :, 0:128].reshape(slots, 128).astype(F32))[:ranks]

    def select(values):
        masked = values * mask
        total = masked[0:RANK]
        for n in range(1, kept):
            total = total + masked[n * RANK:(n + 1) * RANK]
        return total

    def spread(values):
        return jnp.concatenate([values] * kept, axis=0) * mask

    x_rows = x_recv[:, :, 128:].reshape(slots, width)
    low_recv[tme, 0:RANK] = select(dot_nt(ag[...], x_rows))
    low_recv[tme, RANK:2 * RANK] = select(dot_nt(au[...], x_rows))
    def exchange(which, buffer):
        for d in range(1, nt):
            tensor_copy(which, buffer, d).start()
        for d in range(1, nt):
            tensor_copy(which, buffer, d).wait_recv()
        return jnp.sum(buffer[...], axis=0)

    low = exchange(0, low_recv)
    sg_t = spread(low[0:RANK].astype(BF16).astype(F32))
    su_t = spread(low[RANK:].astype(BF16).astype(F32))
    sg[...] = jnp.transpose(sg_t).astype(BF16)
    su[...] = jnp.transpose(su_t).astype(BF16)

    def columns(k, j):
        return pl.ds(pl.multiple_of(k * part + j * sub, 128), sub)

    def forward(k, total):
        for d in range(1, dp):
            gu_copy(k, d).wait_recv()

        def forward_sub(j, total):
            at = columns(k, j)

            def piece(n):
                start = pl.multiple_of(n * part + j * sub, 128)
                return gu_recv[k, :, :, pl.ds(start, sub)].reshape(slots, sub).astype(F32)

            gate_full = piece(0) + ADAPTER_SCALE * dot(sg[...], bg[:, at])
            up_full = piece(1) + ADAPTER_SCALE * dot(su[...], bu[:, at])
            logistic = jax.nn.sigmoid(gate_full)
            activated = gate_full * logistic
            hidden = (activated * up_full).astype(BF16)
            acted[:, at] = activated
            up_slope[:, at] = up_full * (logistic * (1.0 + gate_full * (1.0 - logistic)))
            hiddens[:, at] = hidden
            return total + dot_nt(ad[:, at], hidden)

        return lax.fori_loop(0, part // sub, forward_sub, total)

    zero = jnp.zeros((ranks, slots), F32)
    hidden_sums[tme] = select(lax.fori_loop(0, PARTS, forward, zero))
    sh_t = spread(exchange(1, hidden_sums).astype(BF16).astype(F32))
    delta_send[...] = by_device(ADAPTER_SCALE * dot(jnp.transpose(sh_t).astype(BF16), bd[...]))
    for d in range(1, dp):
        delta_copy(d).start()
    delta_recv[me] = delta_send[me]

    for d in range(1, dp):
        cot_copy(d).wait_recv()
    cot_rows = cot_recv[...].reshape(slots, width)
    cot_sums[tme] = select(dot_nt(bd[...], cot_rows))
    sc_t = spread((ADAPTER_SCALE * exchange(2, cot_sums)).astype(BF16).astype(F32))
    sc[...] = jnp.transpose(sc_t).astype(BF16)
    gbd[...] = ADAPTER_SCALE * dot(sh_t.astype(BF16), cot_rows)
    sg_t, su_t, sc_t = sg_t.astype(BF16), su_t.astype(BF16), sc_t.astype(BF16)

    def backward(k, totals):
        for d in range(1, dp):
            hid_copy(k, d).wait_recv()

        def backward_sub(j, totals):
            back_g, back_u = totals
            at = columns(k, j)
            arrived = hid_recv[k, :, :, pl.ds(pl.multiple_of(j * sub, 128), sub)].reshape(slots, sub)
            hidden_grad = arrived.astype(F32) + dot(sc[...], ad[:, at])
            gate_grad = (hidden_grad * up_slope[:, at]).astype(BF16)
            up_grad = (hidden_grad * acted[:, at]).astype(BF16)
            gbg[:, at] = ADAPTER_SCALE * dot(sg_t, gate_grad)
            gbu[:, at] = ADAPTER_SCALE * dot(su_t, up_grad)
            gad[:, at] = dot(sc_t, hiddens[:, at])
            return back_g + dot_nt(bg[:, at], gate_grad), back_u + dot_nt(bu[:, at], up_grad)

        return lax.fori_loop(0, part // sub, backward_sub, totals)

    back_g, back_u = lax.fori_loop(0, PARTS, backward, (zero, zero))
    back_recv[tme, 0:RANK] = select(back_g)
    back_recv[tme, RANK:] = select(back_u)
    back = ADAPTER_SCALE * exchange(3, back_recv)
    sbg_t = spread(back[0:RANK].astype(BF16).astype(F32))
    sbu_t = spread(back[RANK:].astype(BF16).astype(F32))
    sbg = jnp.transpose(sbg_t).astype(BF16)
    sbu = jnp.transpose(sbu_t).astype(BF16)
    gx_send[...] = by_device(dot(sbg, ag[...]) + dot(sbu, au[...]))
    for d in range(1, dp):
        gx_copy(d).start()
    gx_recv[me] = gx_send[me]
    x_rows = x_recv[:, :, 128:].reshape(slots, width)
    gag[...] = dot(sbg_t.astype(BF16), x_rows)
    gau[...] = dot(sbu_t.astype(BF16), x_rows)
    for d in range(1, dp):
        delta_copy(d).wait_recv()
    delta[...] = dot(place_t[...], delta_recv[...].reshape(slots, width)).astype(BF16)
    for d in range(1, dp):
        x_copy(d).wait_send()
        cot_copy(d).wait_send()
        delta_copy(d).wait_send()
    for n, buffer in enumerate((low_recv, hidden_sums, cot_sums, back_recv)):
        for d in range(1, nt):
            tensor_copy(n, buffer, d).wait_send()

    @pl.loop(0, PARTS)
    def _(k):
        for d in range(1, dp):
            gu_copy(k, d).wait_send()
            hid_copy(k, d).wait_send()

    for d in range(1, dp):
        gx_copy(d).wait_recv()
    gx[...] = dot(place_t[...], gx_recv[...].reshape(slots, width)).astype(BF16)
    for d in range(1, dp):
        gx_copy(d).wait_send()


def write_out(*refs):
    n = len(refs) // 2
    sems = refs[-1]
    copies = [pltpu.make_async_copy(refs[i], refs[n + i], sems.at[i]) for i in range(n)]
    for copy in copies:
        copy.start()
    for copy in copies:
        copy.wait()


def on_device(
    remaining_members, allotment, sample_module_label, block_source_vectors,
    fixed_switch_projection, fixed_expand_projection, result_adjoint_vectors,
    inner_activation_adjoint, switch_left_matrices, switch_right_matrices,
    expand_left_matrices, expand_right_matrices, contract_left_matrices, contract_right_matrices,
):
    dp, nt = lax.axis_size("dp"), lax.axis_size("tensor")
    rows, width = block_source_vectors.shape
    hidden_units = fixed_switch_projection.shape[1]
    ranks = switch_right_matrices.shape[0]
    cap = max(rows // 8, rows // dp)
    slots = dp * cap
    part = hidden_units // PARTS

    out_forms = [
        ((rows, width), BF16), ((rows, width), BF16),
        ((ranks, width), F32), ((ranks, hidden_units), F32),
        ((ranks, width), F32), ((ranks, hidden_units), F32),
        ((ranks, hidden_units), F32), ((ranks, width), F32),
    ]
    anywhere = pl.BlockSpec(memory_space=pl.ANY)
    whole = pl.BlockSpec(memory_space=pltpu.VMEM)
    dma = pltpu.SemaphoreType.DMA
    outs = pl.pallas_call(
        functools.partial(kernel, (dp, nt, cap)),
        out_shape=[pltpu.VMEM(*form) for form in out_forms],
        in_specs=[anywhere] * 14,
        out_specs=[whole] * 8,
        scratch_shapes=[
            pltpu.VMEM((1, rows), jnp.int32),
            pltpu.VMEM((1, remaining_members.shape[0]), jnp.int32),
            pltpu.VMEM((1, allotment.shape[0]), jnp.int32),
            pltpu.VMEM((rows, width), BF16), pltpu.VMEM((rows, width), BF16),
            pltpu.VMEM((PARTS, rows, 2 * part), BF16), pltpu.VMEM((PARTS, rows, part), BF16),
            pltpu.VMEM((ranks, width), BF16), pltpu.VMEM((ranks, width), BF16),
            pltpu.VMEM((ranks, width), BF16),
            pltpu.VMEM((ranks, hidden_units), BF16), pltpu.VMEM((ranks, hidden_units), BF16),
            pltpu.VMEM((ranks, hidden_units), BF16),
            pltpu.VMEM((dp, cap, 128 + width), BF16), pltpu.VMEM((dp, cap, 128 + width), BF16),
            pltpu.VMEM((dp, cap, width), BF16), pltpu.VMEM((dp, cap, width), BF16),
            pltpu.VMEM((PARTS, dp, cap, 2 * part), BF16), pltpu.VMEM((PARTS, dp, cap, 2 * part), BF16),
            pltpu.VMEM((PARTS, dp, cap, part), BF16), pltpu.VMEM((PARTS, dp, cap, part), BF16),
            pltpu.VMEM((nt, 2 * RANK, slots), F32), pltpu.VMEM((nt, RANK, slots), F32),
            pltpu.VMEM((nt, RANK, slots), F32), pltpu.VMEM((nt, 2 * RANK, slots), F32),
            pltpu.VMEM((dp, cap, width), BF16), pltpu.VMEM((dp, cap, width), BF16),
            pltpu.VMEM((dp, cap, width), BF16), pltpu.VMEM((dp, cap, width), BF16),
            pltpu.VMEM((slots, hidden_units), F32), pltpu.VMEM((slots, hidden_units), F32),
            pltpu.VMEM((slots, hidden_units), BF16),
            pltpu.VMEM((slots, rows), BF16), pltpu.VMEM((rows, slots), BF16),
            pltpu.VMEM((slots, ranks), BF16), pltpu.VMEM((slots, ranks), BF16),
            pltpu.VMEM((slots, ranks), BF16),
            dma((11,)), dma((3, PARTS)),
            dma((4, dp)), dma((4, dp)), dma((2, PARTS, dp)), dma((2, PARTS, dp)),
            dma((4, nt)), dma((4, nt)),
        ],
        compiler_params=pltpu.CompilerParams(
            collective_id=0, has_side_effects=True, vmem_limit_bytes=38 * 2**20
        ),
        cost_estimate=pl.CostEstimate(flops=3 * 10**9, bytes_accessed=20 * 2**20, transcendentals=10**6),
    )(
        *[pltpu.with_memory_space_constraint(value, pltpu.HBM) for value in (
            sample_module_label.reshape(1, -1), remaining_members.reshape(1, -1), allotment.reshape(1, -1),
            block_source_vectors, fixed_switch_projection, fixed_expand_projection,
            result_adjoint_vectors, inner_activation_adjoint,
            switch_left_matrices.T, switch_right_matrices, expand_left_matrices.T,
            expand_right_matrices, contract_left_matrices.T, contract_right_matrices,
        )],
    )
    delta, gx, gag, gbg, gau, gbu, gad, gbd = pl.pallas_call(
        write_out,
        out_shape=[jax.ShapeDtypeStruct(*form) for form in out_forms],
        in_specs=[whole] * 8,
        out_specs=[anywhere] * 8,
        scratch_shapes=[dma((8,))],
        compiler_params=pltpu.CompilerParams(vmem_limit_bytes=2 * 2**20),
    )(*[pltpu.with_memory_space_constraint(value, pltpu.VMEM) for value in outs])
    return delta, gx, gag.T, gbg, gau.T, gbu, gad.T, gbd


def solution(mesh):
    rows = P(("groups", "dp"), "tensor")
    left = P(("groups", "tensor"), "dp")
    in_specs = (
        P("groups"), P("groups"), P(("groups", "dp")),
        rows, rows, rows, rows, rows,
        left, rows, left, rows, left, rows,
    )
    out_specs = (rows, rows, left, rows, left, rows, left, rows)
    return jax.shard_map(
        on_device, mesh=mesh, in_specs=in_specs, out_specs=out_specs, check_vma=False
    )
```

time: 191 us -> 176 us (0.921)
  local copies, waits for them, and re-layouts: 12.5 us -> 0 us
  Pallas kernels: 178 us -> 175 us
    unnamed x18 -> x0, local copies, waits for them, and re-layouts: 12.5 us -> none
    pallas_call x1 -> x2, Pallas kernels: 178 us -> 175 us  [the longest x1 172 us: on_device(): pl.pallas_call(functools.partial(kernel, (dp, nt, cap)), out_shape=[pltpu...]
where the time goes in v2:
time: 176 us
  Pallas kernels  175 us (99%)
    pallas_call x1, Pallas kernels, on_device(): pl.pallas_call(functools.partial(kernel, (dp, nt, cap)), out_shape=[pltpu...  172 us

profile of v2, /device:TPU:24, one launch (start us, length us, event | category | flops | bytes accessed | tf_op | source)
XLA Modules:
  0.0 175.5 jit_solution(7193614034398464315)
XLA Ops:
  0.6 171.5 %shard_map.197 = (bf16[128,2048]{1,0:T(8,128)(2,1)S(1)}, bf16[128,2048]{1,0:T(8,128)(2,1)S(1)}, f32[64,2048]{1,0:T(8,128)S(1)}, f32[64,7168]{1,0:T(8,128)S(1)}, ...) custom-call(s32[1,128]{1,0:T(1,128)} %bitcast.15, ...), custom_call_target="tpu_custom_call" | custom-call | flops 3000000000 | bytes 20971520 | tf_op jit(solution)/shard_map/pallas_call | solution.py:377
  172.2 3.3 %shard_map.198 = (bf16[128,2048]{1,0:T(8,128)(2,1)}, bf16[128,2048]{1,0:T(8,128)(2,1)}, f32[64,2048]{1,0:T(8,128)}, f32[64,7168]{1,0:T(8,128)}, f32[64,2048]{1,0...) custom-call(bf16[128,2048]{1,0:T(8,128)(2,1)S(1)} %get-tuple-element.24.refs_0_, ...), custom_call_target="tpu_custom_call" | custom-call | tf_op jit(solution)/shard_map/pallas_call | solution.py:422
